TPU v7x, 128 devices: a whole 4x4x4 slice. The times are simulated.
128 devices in a mesh: teacher: 16 (over z, x), student: 8 (over y, core).
Axes of the slice: x: 4, y: 4, z: 4, core: 2. Of those that a mesh axis runs over, the one named last changes fastest.
Arguments:
- embeddings: bfloat16 [131072, 1024], P(('teacher', 'student')), may hold values from -6 to 6
- action_ids: int32 [131072], P(('teacher', 'student')), may hold values from 0 to 15
- segment_ids: int32 [128, 1024], P(('teacher', 'student')), may hold values from 0 to 7, never falling along the last dimension, each value on 1 to 512 neighbouring positions
- cand_pos: int32 [32768], P(('teacher', 'student')), may hold values from 0 to 1023
- owners: int32 [32768, 1], P(('teacher', 'student')), may hold values from 0 to 15; in each aligned block of 256 rows (0 to 255, 256 to 511, ...) at most 32 rows name the same one
- features: bfloat16 [32768, 512], P(('teacher', 'student')), may hold values from -6 to 6
- action_table: bfloat16 [16, 1024], replicated, may hold values from -3 to 3
- w_query: bfloat16 [1024, 2048], P('teacher'), may hold values from -0.1875 to 0.1875
- w_keys: bfloat16 [1024, 2048], P('teacher'), may hold values from -0.1875 to 0.1875
- w_out: bfloat16 [1024, 1024], P('teacher'), may hold values from -0.1875 to 0.1875
- w_head: bfloat16 [1024, 128], replicated, may hold values from -0.1875 to 0.1875
- w_cross: bfloat16 [512, 512], replicated, may hold values from -0.25 to 0.25
- b_cross: bfloat16 [512], replicated, may hold values from -3 to 3
- w_deep: bfloat16 [512, 4096], replicated, may hold values from -0.25 to 0.25
- b_deep: bfloat16 [4096], replicated, may hold values from -3 to 3
- w_score: bfloat16 [4096, 128], replicated, may hold values from -0.09375 to 0.09375
- b_score: bfloat16 [128], replicated, may hold values from -3 to 3
Outputs:
- grad_cross: float32 [512, 512], P(('teacher', 'student'))
- grad_bcross: float32 [512], P(('teacher', 'student'))
- grad_deep: float32 [512, 4096], P(('teacher', 'student'))
- grad_bdeep: float32 [4096], P(('teacher', 'student'))
- grad_score: float32 [4096, 128], P(('teacher', 'student'))
- grad_bscore: float32 [128], P(('teacher', 'student'))
- student_rows: bfloat16 [65536, 128], P(('teacher', 'student'))
Inputs may be any that keep to these rules, and one draw needn't show every extreme that they name: `owners`: within the candidates of one device, no owner is named by more than 32 of them, a bound that some block reaches.
All inputs are finite; a program needn't handle non-finite values.
Results may differ from a plain program's by a relative error of at most 0.012.
Values may be sent and summed in bfloat16 or wider, within the bound.
A program may use at most 128 MiB of HBM per device.

v0:
```python
import functools

import jax
import jax.numpy as jnp
from jax import lax
from jax.experimental import pallas as pl
from jax.experimental.pallas import tpu as pltpu
from jax.sharding import PartitionSpec as P

CAP = 32
EPS = 1e-05
BF = jnp.bfloat16
F32 = jnp.float32
MESH = pl.DeviceIdType.MESH

ROUTES = ((0, 1, 2), (1, 2, 0), (2, 0, 1))


def nn(a, b):
    return lax.dot_general(a, b, (((1,), (0,)), ((), ())), preferred_element_type=F32)


def nt(a, b):
    return lax.dot_general(a, b, (((1,), (1,)), ((), ())), preferred_element_type=F32)


def silu(v):
    half = 0.5 * v
    return half + half * jnp.tanh(half)


def flip(v):
    return v.astype(F32).T.astype(BF)


def kernel(
    emb_hbm,
    ids_ref,
    segs_ref,
    cand_ref,
    owners_ref,
    feat_ref,
    table_ref,
    w_query_hbm,
    w_keys_hbm,
    w_out_ref,
    w_head_ref,
    w_cross_ref,
    b_cross_ref,
    w_deep_hbm,
    b_deep_ref,
    w_score_hbm,
    b_score_ref,
    o_cross,
    o_deep,
    o_score,
    o_bias,
    o_rows,
    emb,
    w_deep_ref,
    w_score_ref,
    heads,
    out_head,
    own_half,
    table_pad,
    hist,
    picked,
    mask,
    kv,
    gate,
    gate_out,
    mixed,
    mixed_out,
    joined,
    base,
    crossed,
    ct,
    ct_sib,
    ft,
    ft_sib,
    hid_t,
    slope,
    scores,
    place_out,
    rows_in,
    d_own,
    d_sib,
    gs,
    gs_sib,
    dc,
    dc_sib,
    bd,
    grads,
    x1,
    x2,
    x3,
    y3,
    w1,
    v1,
    w2,
    last,
    fin,
    s1s,
    s1r,
    s2s,
    s2r,
    s3s,
    s3r,
    scs,
    scr,
    srs,
    srr,
    lds,
    hds,
    p1s,
    p1r,
    p2s,
    p2r,
    ups,
    upr,
    sbs,
    sbr,
    ohs,
    ohr,
):
    t = lax.axis_index("teacher")
    s = lax.axis_index("student")
    z, x = t // 4, t % 4
    y, c = s // 2, s % 2
    pos = (z, x, y)
    sibling = (t, y * 2 + 1 - c)
    sends = []

    def at_chip(axis, value, core):
        p = list(pos)
        p[axis] = value
        return (p[0] * 4 + p[1], p[2] * 2 + core)

    def push(src, dst, send_sem, recv_sem, device):
        copy = pltpu.make_async_remote_copy(
            src_ref=src,
            dst_ref=dst,
            send_sem=send_sem,
            recv_sem=recv_sem,
            device_id=device,
            device_id_type=MESH,
        )
        copy.start()
        sends.append(copy)
        return copy

    peers = [((t + k) % 16, s) for k in range(1, 16)] + [sibling]
    peers += [at_chip(2, (y + k) % 4, c) for k in range(1, 4)]
    peers += [at_chip(axis, (pos[axis] + k) % 4, 1 - c) for axis in range(3) for k in range(1, 4)]
    barrier = pltpu.get_barrier_semaphore()
    for peer in peers:
        pl.semaphore_signal(barrier, inc=1, device_id=peer, device_id_type=MESH)

    odd = y % 2
    first = (1 - c) * x + c * z
    second = (1 - c) * z + c * x

    def shard(i, j):
        i, j = (first + i) % 4, (second + j) % 4
        return (1 - c) * (j * 4 + i) + c * (i * 4 + j)

    def head_of(k, core):
        return (4 + 2 * odd + core, core, 2 + core, 6 - 2 * odd + core)[k]

    own_cols = []
    for k in range(3):
        for part, (ref, start) in enumerate(
            ((w_keys_hbm, 0), (w_keys_hbm, 1024), (w_query_hbm, 0), (w_query_hbm, 1024))
        ):
            cols = pl.ds(pl.multiple_of(start + head_of(k, c) * 128, 128), 128)
            own_cols.append(
                pltpu.make_async_copy(
                    ref.at[:, cols],
                    heads.at[k, t, :, 128 * part : 128 * part + 128],
                    hds.at[k, part],
                )
            )
            own_cols[-1].start()
    loads = [
        pltpu.make_async_copy(w_deep_hbm, w_deep_ref, lds.at[0]),
        pltpu.make_async_copy(w_score_hbm, w_score_ref, lds.at[1]),
        pltpu.make_async_copy(emb_hbm, emb, lds.at[2]),
    ]
    for load in loads:
        load.start()

    def along(k, i, j, rows, send_sem, recv_sem, device):
        ref = heads.at[k, shard(i, j), rows]
        return push(ref, ref, send_sem, recv_sem, device)

    full = slice(0, 64)
    y_next = (t, (y + 1 + 2 * c) % 4 * 2 + c)
    p1, p2, ups_done = {}, {}, []

    def to_y(k, i, j):
        if k == 0:
            n = (i % 4) * 4 + j % 4
            up = heads.at[0, shard(i, j)]
            ups_done.append(push(up, heads.at[3, shard(i, j)], ups.at[n], upr.at[n], y_next))

    def spread(k, i):
        for side, step in enumerate((1, 3, 2) if k == 0 else (1, 3)):
            device = (shard(0, step), s)
            p2[k, i, side] = along(k, i, 0, full, p2s.at[k, i, side], p2r.at[k, i, side], device)
        to_y(k, i, 0)

    def hop(k):
        for side, step in enumerate((1, 3, 2)):
            device = (shard(step, 0), s)
            p1[k, side] = along(k, 0, 0, full, p1s.at[k, side], p1r.at[k, side], device)

    def hop_end(k):
        for side in range(3):
            p1[k, side].wait_recv()

    def arrive(i):
        for side, j in enumerate((3, 1, 2)):
            p2[0, i, side].wait_recv()
            to_y(0, i, j)

    def event3(k):
        for i in (0, 1, 3, 2):
            side = 0 if i < 2 else 1
            step = (1, 3)[side]
            p2[k, i, side].wait_recv()
            device = (shard(0, step), s)
            p2[k, i, 2] = along(k, i, 4 - step, full, p2s.at[k, i, 2], p2r.at[k, i, 2], device)
            p2[k, i, 1 - side].wait_recv()

    def event4(k):
        for i in range(4):
            p2[k, i, 2].wait_recv()

    for copy in own_cols:
        copy.wait()
    pl.semaphore_wait(barrier, len(peers))
    hop(0)
    spread(0, 0)
    hop(1)
    hop(2)

    feats = feat_ref[...]
    feats32 = feats.astype(F32)
    cross = nn(feats, w_cross_ref[...]) + b_cross_ref[...].astype(F32).reshape(1, 512)
    crossed[...] = (feats32 * cross + feats32).astype(BF)
    ct[...] = flip(crossed[...])
    ft[...] = flip(feats)
    ct_copy = push(ct, ct_sib, scs.at[0], scr.at[0], sibling)
    ft_copy = push(ft, ft_sib, scs.at[1], scr.at[1], sibling)
    scores[...] = jnp.broadcast_to(b_score_ref[...].astype(F32), scores.shape)
    table_pad[...] = jnp.zeros_like(table_pad)
    table_pad[0:16] = table_ref[...]
    loads[2].wait()

    def embed(i):
        rows = slice(i * 256, i * 256 + 256)
        kinds = lax.broadcasted_iota(jnp.int32, (128, 256), 0)
        onehot = flip(kinds == ids_ref[:, rows])
        hist[0, rows, :] = (emb[rows, :].astype(F32) + nn(onehot, table_pad[...])).astype(BF)

    for i in range(4):
        embed(i)
    hist_copy = push(hist.at[0], hist.at[1], sbs.at[0], sbr.at[0], sibling)
    hop_end(0)
    for i in (3, 1, 2):
        spread(0, i)
    b_deep32 = b_deep_ref[...].astype(F32).reshape(1, 4096)

    def forward(j):
        cols = slice(j * 512, j * 512 + 512)
        pre = nn(crossed[...], w_deep_ref[:, cols]) + b_deep32[:, cols]
        sigma = 0.5 + 0.5 * jnp.tanh(0.5 * pre)
        hidden = (pre * sigma).astype(BF)
        slope[j] = sigma * (1.0 + pre * (1.0 - sigma))
        hid_t[cols, :] = hidden.T
        scores[...] += nn(hidden, w_score_ref[cols, :])

    loads[0].wait()
    loads[1].wait()
    for j in range(2):
        forward(j)
    for k in (1, 2):
        hop_end(k)
        for i in range(4):
            spread(k, i)

    where_col = jnp.broadcast_to(cand_ref[...], (128, 256)).astype(F32).T[:, 0:1]
    places = lax.broadcasted_iota(jnp.int32, (256, 1024), 1).astype(F32)
    segs = segs_ref[...].astype(F32)
    chosen = (places == where_col).astype(F32)
    picked[0:256] = nn(chosen.astype(BF), hist[0]).astype(BF)
    seg_col = jnp.sum(chosen * segs, axis=1, keepdims=True)
    mask[0] = jnp.where((segs == seg_col) & (places <= where_col), 1.0, 0.0)
    base[...] = nn(picked[0:256], w_head_ref[...])
    picked_copy = push(picked.at[0:256], picked.at[256:512], sbs.at[1], sbr.at[1], sibling)
    mask_copy = push(mask.at[0], mask.at[1], sbs.at[2], sbr.at[2], sibling)
    arrive(0)
    for j in range(2, 5):
        forward(j)
    arrive(3)
    arrive(1)
    for j in range(5, 8):
        forward(j)
    arrive(2)

    att_done = []

    def attend(k, between=None):
        head = head_of(k, c)
        columns = heads[k].reshape(1024, 512)
        qrows = silu(nn(picked[...], columns[:, 256:512])).astype(BF)
        gate[head] = qrows[:256, :128]
        gate_out[k] = qrows[256:, :128]
        for side in (1, 0):
            kv[side] = silu(nn(hist[side], columns[:, :256])).astype(BF)
        if between is not None:
            between()
        for side in (1, 0):
            half = nt(qrows[256 * side : 256 * side + 256, 128:], kv[side, :, 128:])
            half = half * (0.5 * 128 ** (-0.5))
            weights = ((half + half * jnp.tanh(half)) * mask[side]).astype(BF)
            result = nn(weights, kv[side, :, :128])
            if side == 0:
                mixed[head] = result
            else:
                mixed_out[k] = result
                for n, (src, dst) in enumerate(((mixed_out, mixed), (gate_out, gate))):
                    n += 3 + 2 * k
                    att_done.append(push(src.at[k], dst.at[head], sbs.at[n], sbr.at[n], sibling))

    dest = owners_ref[...]
    kinds = lax.broadcasted_iota(jnp.int32, (16, 256), 0)
    hits = (kinds == dest).astype(F32)
    upper = (
        lax.broadcasted_iota(jnp.int32, (256, 256), 0)
        < lax.broadcasted_iota(jnp.int32, (256, 256), 1)
    ).astype(BF)
    before = nn(hits.astype(BF), upper)
    rank = jnp.sum(before * hits, axis=0, keepdims=True).astype(jnp.int32)
    slot = dest * CAP + rank
    place = (lax.broadcasted_iota(jnp.int32, (512, 256), 0) == slot).astype(BF)
    own_out = nn(w_out_ref[...], w_head_ref[...]).astype(BF)
    own_half[...] = own_out
    mine_rows = pl.ds(pl.multiple_of(32 * c, 32), 32)
    placed = nn(place, scores[...].astype(BF)).astype(BF).reshape(16, CAP, 128)
    place_out[:, :CAP] = placed
    place_out[:, CAP:] = jnp.broadcast_to(own_half[mine_rows, :][None], (16, 32, 128))
    rows_in[t] = place_out[t]
    row_copies = []
    for k in range(1, 16):
        to = (t + k) % 16
        row_copies.append(push(place_out.at[to], rows_in.at[t], srs.at[k], srr.at[k], (to, s)))

    event3(1)
    for copy in (hist_copy, picked_copy, mask_copy):
        copy.wait_recv()
    attend(0, functools.partial(event3, 2))
    event4(1)
    attend(1, functools.partial(event4, 2))
    for copy in row_copies:
        copy.wait_recv()
    out_head[:, mine_rows] = rows_in[:, CAP:]
    every = out_head.at[:, mine_rows]
    oh_sib = push(every, every, ohs.at[0], ohr.at[0], sibling)
    attend(2)
    for copy in ups_done:
        copy.wait_recv()
    attend(3)
    for copy in att_done:
        copy.wait_recv()

    centre = jnp.sum(jnp.sum(mixed[...], axis=0), axis=1, keepdims=True) * (1.0 / 1024.0)
    spread_sum = jnp.sum(jnp.square(mixed[...] - centre[None]), axis=0)
    scale_rows = lax.rsqrt(jnp.sum(spread_sum, axis=1, keepdims=True) * (1.0 / 1024.0) + EPS)
    for head in range(8):
        normed = (mixed[head] - centre) * scale_rows
        joined[:, 128 * head : 128 * head + 128] = (normed * gate[head].astype(F32)).astype(BF)
    oh_sib.wait_recv()
    logits = base[...] + nn(joined[...], out_head[...].reshape(1024, 128))

    delta = scores[...] - logits.astype(BF).astype(F32)
    delta16 = delta.astype(BF)
    bscore = jnp.sum(delta, axis=0, keepdims=True)

    def back_chunk(j):
        rows = pl.ds(pl.multiple_of(j * 512, 512), 512)
        dpre = nt(delta16, w_score_ref[rows, :]) * slope[j]
        d_own[j] = dpre.astype(BF)
        bd[j] = jnp.broadcast_to(jnp.sum(dpre, axis=0, keepdims=True), (8, 512))

    d_copies = {}
    for q in (0, 1, 3, 2):
        j = (1 - c) * 4 + q
        back_chunk(j)
        d_copies[q] = push(d_own.at[j], d_sib.at[q], scs.at[2 + q], scr.at[2 + q], sibling)
    for q in (0, 1, 3, 2):
        back_chunk(c * 4 + q)
    for i in range(8):
        g = nn(hid_t[512 * i : 512 * i + 512, :], delta16).astype(BF).reshape(8, 2, 2, 16, 128)
        for core in range(2):
            gs[core, 8 * i : 8 * i + 8, :, 0:128] = g[:, core, 0]
            gs[core, 8 * i : 8 * i + 8, :, 128:256] = g[:, core, 1]
    gs_copy = push(gs.at[1 - c], gs_sib, scs.at[6], scr.at[6], sibling)
    every_dpre = jnp.concatenate([d_own[j] for j in range(8)], axis=1)
    dcr = nt(every_dpre, w_deep_ref[...]) * feats32
    bcross = jnp.sum(dcr, axis=0, keepdims=True)
    dc[0] = dcr[:, :256].astype(BF)
    dc[1] = dcr[:, 256:].astype(BF)
    dc_copy = push(dc.at[1 - c], dc_sib, scs.at[7], scr.at[7], sibling)

    def axes_of(u):
        axis = ROUTES[u // 2][0]
        rest = [a for a in range(3) if a != axis]
        return axis, rest

    def piece(u, where, half):
        axis, rest = axes_of(u)
        index = [slice(None)] * 3
        index[axis] = where
        index[rest[0]] = pl.ds(2 * half, 2)
        return (u, *index)

    def stage1_first(u):
        axis, _ = axes_of(u)
        m = pos[axis]
        right, left, opp = (m + 1) % 4, (m + 3) % 4, (m + 2) % 4
        to_right, to_left = at_chip(axis, right, c), at_chip(axis, left, c)
        return (
            push(grads.at[piece(u, opp, 0)], x1.at[u, 0], s1s.at[u, 0], s1r.at[u, 0], to_right),
            push(grads.at[piece(u, opp, 1)], x1.at[u, 1], s1s.at[u, 1], s1r.at[u, 1], to_left),
        )

    def stage1_second(u):
        axis, _ = axes_of(u)
        m = pos[axis]
        right, left = (m + 1) % 4, (m + 3) % 4
        to_right, to_left = at_chip(axis, right, c), at_chip(axis, left, c)
        return (
            push(grads.at[piece(u, right, 1)], x2.at[u, 0], s1s.at[u, 2], s1r.at[u, 2], to_right),
            push(grads.at[piece(u, left, 0)], x2.at[u, 1], s1s.at[u, 3], s1r.at[u, 3], to_left),
        )

    def stage1_pass(u, started):
        axis, _ = axes_of(u)
        m = pos[axis]
        right, left = (m + 1) % 4, (m + 3) % 4
        out = []
        for side, (where, device) in enumerate(
            ((right, at_chip(axis, right, c)), (left, at_chip(axis, left, c)))
        ):
            started[side].wait_recv()
            mine = grads[piece(u, where, side)].astype(F32)
            y3[u, side] = (mine + x1[u, side].astype(F32)).astype(BF)
            out.append(
                push(y3.at[u, side], x3.at[u, side], s1s.at[u, 4 + side], s1r.at[u, 4 + side], device)
            )
        return out

    def stage1_end(u, started, passed):
        axis, _ = axes_of(u)
        m = pos[axis]
        for copy in (started[2], started[3], passed[0], passed[1]):
            copy.wait_recv()
        for half in range(2):
            total = grads[piece(u, m, half)].astype(F32)
            total += x2[u, 1 - half].astype(F32) + x3[u, half].astype(F32)
            w1[u // 2, u % 2, 2 * half : 2 * half + 2] = total.astype(BF)

    started, passed = {}, {}

    ct_copy.wait_recv()
    for q in (0, 1, 3, 2):
        d_copies[q].wait_recv()
        g = nn(ct[...], d_own[c * 4 + q]) + nn(ct_sib[...], d_sib[q])
        g = g.reshape(64, 8, 512)
        g = jnp.concatenate([g[:, :, :256], g[:, :, 256:]], axis=1)
        grads[1 + q] = g.astype(BF).reshape(4, 4, 4, 16, 256)
        started[1 + q] = stage1_first(1 + q)

    gs_copy.wait_recv()
    summed = gs[c].astype(F32) + gs_sib[...].astype(F32)
    grads[0] = summed.astype(BF).reshape(4, 4, 4, 16, 256)
    started[0] = stage1_first(0)

    for u in (1, 2, 4):
        started[u] += stage1_second(u)

    sub = lax.broadcasted_iota(jnp.int32, (16, 128), 0)
    for pair in range(32):
        deep_row = bd[pair // 4, 0:1, (pair % 4) * 128 : (pair % 4) * 128 + 128]
        cross_row = bcross[:, (pair // 8) * 128 : (pair // 8) * 128 + 128]
        tile = jnp.where(sub == 0, deep_row, jnp.where(sub == 1, cross_row, bscore))
        tile = tile.astype(BF)
        for chip in (2 * pair, 2 * pair + 1):
            grads[5, chip // 16, chip // 4 % 4, chip % 4, :, 128:256] = tile
    ft_copy.wait_recv()
    dc_copy.wait_recv()
    g = nn(ft[...], dc[c]) + nn(ft_sib[...], dc_sib[...])
    g = g.reshape(64, 8, 256)
    g = jnp.concatenate([g[:, :, :128], g[:, :, 128:]], axis=1)
    grads[5, :, :, :, :, 0:128] = g.astype(BF).reshape(4, 4, 4, 16, 128)
    started[5] = stage1_first(5)
    for u in (3, 0, 5):
        started[u] += stage1_second(u)
    for u in (1, 2, 4, 3, 0, 5):
        passed[u] = stage1_pass(u, started[u])

    def piece2(u, where):
        axis, second, _ = ROUTES[u // 2]
        rest = [a for a in range(3) if a != axis]
        index = [slice(None)] * 2
        index[rest.index(second)] = where
        return (u // 2, u % 2, *index)

    def stage2_start(u):
        axis = ROUTES[u // 2][1]
        m = pos[axis]
        return [
            push(
                w1.at[piece2(u, (m + step) % 4)],
                v1.at[u, k],
                s2s.at[u, k],
                s2r.at[u, k],
                at_chip(axis, (m + step) % 4, c),
            )
            for k, step in enumerate((1, 3, 2))
        ]

    def stage2_end(u, begun):
        total = w1[piece2(u, pos[ROUTES[u // 2][1]])].astype(F32)
        for k, copy in enumerate(begun):
            copy.wait_recv()
            total += v1[u, k].astype(F32)
        w2[u // 2, u % 2] = total.astype(BF)

    def stage3_start(r):
        axis = ROUTES[r][2]
        m = pos[axis]
        last[r, m, c] = w2[r, :, m]
        for k in range(4):
            where = (m + k) % 4
            for other in range(2):
                if k == 0 and other == 0:
                    continue
                core = c if other == 0 else 1 - c
                push(
                    w2.at[r, :, where],
                    last.at[r, m, c],
                    s3s.at[r, k, other],
                    s3r.at[r, k, other],
                    at_chip(axis, where, core),
                )

    def stage3_end(r):
        axis = ROUTES[r][2]
        m = pos[axis]
        for k in range(4):
            where = (m + 4 - k) % 4
            for other in range(2):
                if k == 0 and other == 0:
                    continue
                core = c if other == 0 else 1 - c
                pltpu.make_async_remote_copy(
                    src_ref=last.at[r, where, core],
                    dst_ref=last.at[r, where, core],
                    send_sem=s3s.at[r, k, other],
                    recv_sem=s3r.at[r, k, other],
                    device_id=at_chip(axis, where, core),
                    device_id_type=MESH,
                ).wait_recv()
        scale = 1.0 / 32768.0
        for core in range(2):
            total = last[r, 0, core].astype(F32)
            for k in range(1, 4):
                total += last[r, k, core].astype(F32)
            fin[core, 2 * r : 2 * r + 2] = total * scale

    begun = {}
    for u in (1, 2, 4, 3, 0, 5):
        stage1_end(u, started[u], passed[u])
        begun[u] = stage2_start(u)
    for r in range(3):
        for u in (2 * r, 2 * r + 1):
            stage2_end(u, begun[u])
        stage3_start(r)
    o_rows[...] = rows_in[:, :CAP]
    for r in range(3):
        stage3_end(r)

    def own_rows(core, unit, half, cols):
        lower = fin[core, unit, 8 * half : 8 * half + 4, cols]
        higher = fin[core, unit, 8 * half + 4 : 8 * half + 8, cols]
        return jnp.where(c == 0, lower, higher)

    for core in range(2):
        for half in range(2):
            for q in range(4):
                at = core * 2048 + q * 512 + half * 256
                o_deep[:, at : at + 256] = own_rows(core, 1 + q, half, slice(0, 256))
            at = core * 256 + half * 128
            o_cross[:, at : at + 128] = own_rows(core, 5, half, slice(0, 128))
    for half in range(2):
        cols = slice(128 * half, 128 * half + 128)
        o_score[16 * half : 16 * half + 16] = jnp.where(c == 0, fin[0, 0, :, cols], fin[1, 0, :, cols])
    chip = t * 4 + y
    bias = fin[0, 5, 0:8, 128:256] + fin[1, 5, 0:8, 128:256]
    for row, first in enumerate((chip % 2 * 64 + c * 32, chip % 16 * 8 + c * 4, chip * 2 + c)):
        o_bias[row : row + 1] = pltpu.roll(bias, (128 - first) % 128, 1)[row : row + 1]
    for copy in sends:
        copy.wait_send()


def results(cross, deep, score, bias, rows, o_cross, o_bcross, o_deep, o_bdeep, o_score, o_bscore, o_rows):
    o_cross[...] = cross[...]
    o_deep[...] = deep[...]
    o_score[...] = score[...]
    o_rows[...] = rows[...]
    o_bdeep[...] = bias[0, 0:32]
    o_bcross[...] = bias[1, 0:4]
    o_bscore[...] = bias[2, 0:1]


def local(
    embeddings,
    action_ids,
    segment_ids,
    cand_pos,
    owners,
    features,
    action_table,
    w_query,
    w_keys,
    w_out,
    w_head,
    w_cross,
    b_cross,
    w_deep,
    b_deep,
    w_score,
    b_score,
):
    dma = pltpu.SemaphoreType.DMA
    vmem = pltpu.VMEM
    whole = pl.BlockSpec(memory_space=pltpu.VMEM)
    stay = pl.BlockSpec(memory_space=pl.ANY)
    g_cross, g_deep, g_score, bias, rows = pl.pallas_call(
        kernel,
        out_shape=(
            jax.ShapeDtypeStruct((4, 512), F32),
            jax.ShapeDtypeStruct((4, 4096), F32),
            jax.ShapeDtypeStruct((32, 128), F32),
            jax.ShapeDtypeStruct((8, 128), F32),
            jax.ShapeDtypeStruct((16, CAP, 128), BF),
        ),
        in_specs=[stay] + [whole] * 6 + [stay] * 2 + [whole] * 4 + [stay, whole, stay, whole],
        out_specs=(whole,) * 5,
        scratch_shapes=[
            vmem((1024, 1024), BF),
            vmem((512, 4096), BF),
            vmem((4096, 128), BF),
            vmem((4, 16, 64, 512), BF),
            vmem((16, 64, 128), BF),
            vmem((64, 128), BF),
            vmem((128, 1024), BF),
            vmem((2, 1024, 1024), BF),
            vmem((512, 1024), BF),
            vmem((2, 256, 1024), F32),
            vmem((2, 1024, 256), BF),
            vmem((8, 256, 128), BF),
            vmem((4, 256, 128), BF),
            vmem((8, 256, 128), F32),
            vmem((4, 256, 128), F32),
            vmem((256, 1024), BF),
            vmem((256, 128), F32),
            vmem((256, 512), BF),
            vmem((512, 256), BF),
            vmem((512, 256), BF),
            vmem((512, 256), BF),
            vmem((512, 256), BF),
            vmem((4096, 256), BF),
            vmem((8, 256, 512), F32),
            vmem((256, 128), F32),
            vmem((16, CAP + 32, 128), BF),
            vmem((16, CAP + 32, 128), BF),
            vmem((8, 256, 512), BF),
            vmem((4, 256, 512), BF),
            vmem((2, 64, 16, 256), BF),
            vmem((64, 16, 256), BF),
            vmem((2, 256, 256), BF),
            vmem((256, 256), BF),
            vmem((8, 8, 512), F32),
            vmem((6, 4, 4, 4, 16, 256), BF),
            vmem((6, 2, 2, 4, 16, 256), BF),
            vmem((6, 2, 2, 4, 16, 256), BF),
            vmem((6, 2, 2, 4, 16, 256), BF),
            vmem((6, 2, 2, 4, 16, 256), BF),
            vmem((3, 2, 4, 4, 16, 256), BF),
            vmem((6, 3, 4, 16, 256), BF),
            vmem((3, 2, 4, 16, 256), BF),
            vmem((3, 4, 2, 2, 16, 256), BF),
            vmem((2, 6, 16, 256), F32),
            dma((6, 6)),
            dma((6, 6)),
            dma((6, 3)),
            dma((6, 3)),
            dma((3, 4, 2)),
            dma((3, 4, 2)),
            dma((8,)),
            dma((8,)),
            dma((16,)),
            dma((16,)),
            dma((3,)),
            dma((3, 4)),
            dma((3, 4)),
            dma((3, 4)),
            dma((3, 4, 3)),
            dma((3, 4, 3)),
            dma((16,)),
            dma((16,)),
            dma((11,)),
            dma((11,)),
            dma((1,)),
            dma((1,)),
        ],
        compiler_params=pltpu.CompilerParams(
            collective_id=0, has_side_effects=True, vmem_limit_bytes=56 * 1024 * 1024
        ),
    )(
        embeddings,
        action_ids.reshape(1, -1),
        segment_ids,
        cand_pos.reshape(1, -1),
        owners.reshape(1, -1),
        features,
        action_table,
        w_query,
        w_keys,
        w_out,
        w_head,
        w_cross,
        b_cross,
        w_deep,
        b_deep,
        w_score,
        b_score.reshape(1, -1),
    )
    return pl.pallas_call(
        results,
        out_shape=(
            jax.ShapeDtypeStruct((4, 512), F32),
            jax.ShapeDtypeStruct((4,), F32),
            jax.ShapeDtypeStruct((4, 4096), F32),
            jax.ShapeDtypeStruct((32,), F32),
            jax.ShapeDtypeStruct((32, 128), F32),
            jax.ShapeDtypeStruct((1,), F32),
            jax.ShapeDtypeStruct((512, 128), BF),
        ),
        in_specs=[whole] * 5,
        out_specs=(whole,) * 7,
    )(g_cross, g_deep, g_score, bias, rows.reshape(512, 128))


def solution(mesh):
    both = ("teacher", "student")
    return jax.shard_map(
        local,
        mesh=mesh,
        in_specs=(
            P(both, None),
            P(both),
            P(both, None),
            P(both),
            P(both, None),
            P(both, None),
            P(),
            P("teacher", None),
            P("teacher", None),
            P("teacher", None),
            P(),
            P(),
            P(),
            P(),
            P(),
            P(),
            P(),
        ),
        out_specs=(
            P(both, None),
            P(both),
            P(both, None),
            P(both),
            P(both, None),
            P(both),
            P(both, None),
        ),
        check_vma=False,
    )
```

profile of v0, /device:TPU:1, one launch (start us, length us, event | category | flops | bytes accessed | tf_op | source)
XLA Modules:
  0.0 72.4 jit_solution(12182706139336702278)
XLA Ops:
  0.6 70.0 %shard_map.216 = (f32[4,512]{1,0:T(4,128)}, f32[4,4096]{1,0:T(4,128)}, f32[32,128]{1,0:T(8,128)}, f32[8,128]{1,0:T(8,128)}, bf16[16,32,128]{2,1,0:T(8,128)(2,1)}) custom-call(bf16[1024,1024]{1,0:T(8,128)(2,1)} %emb_hbm.1, s32[1,1024]{1,0:T(1,128)} %bitcast.6, s32[1,1024]{1,0:T(1,128)} %segs_ref.1, s32[1,256]{1,0:T(1,128)} %bitcast.7, s32[1,256]{1,0:T(1,128)} %bitcast.8, ...), custom_call_target="tpu_custom_call" | custom-call | tf_op jit(solution)/shard_map/pallas_call | solution.py:651
  70.7 1.7 %shard_map.217 = (f32[4,512]{1,0:T(4,128)}, f32[4]{0:T(128)}, f32[4,4096]{1,0:T(4,128)}, f32[32]{0:T(128)}, f32[32,128]{1,0:T(8,128)}, /*index=5*/f32[1]{0:T(128)}, bf16[512,128]{1,0:T(8,128)(2,1)}) custom-call(f32[4,512]{1,0:T(4,128)} %get-tuple-element.12.cross, f32[4,4096]{1,0:T(4,128)} %get-tuple-element.13.deep, f32[32,128]{1,0:T(8,128)} %get-tuple-element.14.score, ...), custom_call_target="tpu_custom_call" | custom-call | tf_op jit(solution)/shard_map/pallas_call | solution.py:752
where the time goes:
time: 72.5 us; the launch traced here: 72.4 us
  Pallas kernels  71.7 us (99%)
    pallas_call x1, Pallas kernels, local(): pl.pallas_call(kernel, out_shape=(jax.ShapeDtypeStruct((4, 512), F32), ja...  70 us
    pallas_call x1, Pallas kernels, local(): pl.pallas_call(results, out_shape=(jax.ShapeDtypeStruct((4, 512), F32), j...  1.69 us

commit v1 on v0

--- a/solution.py
+++ b/solution.py
@@ -35,27 +35,39 @@
 
 def kernel(
     emb_hbm,
+    ids_hbm,
+    segs_hbm,
+    cand_hbm,
+    owners_hbm,
+    feat_hbm,
+    table_hbm,
+    w_query_hbm,
+    w_keys_hbm,
+    w_out_hbm,
+    w_head_hbm,
+    w_cross_hbm,
+    b_cross_hbm,
+    w_deep_hbm,
+    b_deep_hbm,
+    w_score_hbm,
+    b_score_hbm,
+    o_cross,
+    o_deep,
+    o_score,
+    o_bias,
+    o_rows,
     ids_ref,
     segs_ref,
     cand_ref,
     owners_ref,
     feat_ref,
     table_ref,
-    w_query_hbm,
-    w_keys_hbm,
     w_out_ref,
     w_head_ref,
     w_cross_ref,
     b_cross_ref,
-    w_deep_hbm,
     b_deep_ref,
-    w_score_hbm,
     b_score_ref,
-    o_cross,
-    o_deep,
-    o_score,
-    o_bias,
-    o_rows,
     emb,
     w_deep_ref,
     w_score_ref,
@@ -136,7 +148,7 @@
         p[axis] = value
         return (p[0] * 4 + p[1], p[2] * 2 + core)
 
-    def push(src, dst, send_sem, recv_sem, device):
+    def push(src, dst, send_sem, recv_sem, device, shared=False):
         copy = pltpu.make_async_remote_copy(
             src_ref=src,
             dst_ref=dst,
@@ -146,8 +158,19 @@
             device_id_type=MESH,
         )
         copy.start()
-        sends.append(copy)
+        if not shared:
+            sends.append(copy)
         return copy
+
+    def whole_of(ref, send_sem, recv_sem):
+        return pltpu.make_async_remote_copy(
+            src_ref=ref,
+            dst_ref=ref,
+            send_sem=send_sem,
+            recv_sem=recv_sem,
+            device_id=sibling,
+            device_id_type=MESH,
+        )
 
     peers = [((t + k) % 16, s) for k in range(1, 16)] + [sibling]
     peers += [at_chip(2, (y + k) % 4, c) for k in range(1, 4)]
@@ -181,38 +204,50 @@
                 )
             )
             own_cols[-1].start()
-    loads = [
-        pltpu.make_async_copy(w_deep_hbm, w_deep_ref, lds.at[0]),
-        pltpu.make_async_copy(w_score_hbm, w_score_ref, lds.at[1]),
-        pltpu.make_async_copy(emb_hbm, emb, lds.at[2]),
-    ]
+    pairs = (
+        (feat_hbm, feat_ref),
+        (w_cross_hbm, w_cross_ref),
+        (b_cross_hbm, b_cross_ref),
+        (b_score_hbm, b_score_ref),
+        (ids_hbm, ids_ref),
+        (table_hbm, table_ref),
+        (segs_hbm, segs_ref),
+        (cand_hbm, cand_ref),
+        (owners_hbm, owners_ref),
+        (w_out_hbm, w_out_ref),
+        (w_head_hbm, w_head_ref),
+        (b_deep_hbm, b_deep_ref),
+        (w_deep_hbm, w_deep_ref),
+        (w_score_hbm, w_score_ref),
+        (emb_hbm, emb),
+    )
+    loads = [pltpu.make_async_copy(src, dst, lds.at[n]) for n, (src, dst) in enumerate(pairs)]
     for load in loads:
         load.start()
 
     def along(k, i, j, rows, send_sem, recv_sem, device):
         ref = heads.at[k, shard(i, j), rows]
-        return push(ref, ref, send_sem, recv_sem, device)
+        return push(ref, ref, send_sem, recv_sem, device, True)
 
     full = slice(0, 64)
     y_next = (t, (y + 1 + 2 * c) % 4 * 2 + c)
-    p1, p2, ups_done = {}, {}, []
+    p1, p2 = {}, {}
 
     def to_y(k, i, j):
         if k == 0:
-            n = (i % 4) * 4 + j % 4
             up = heads.at[0, shard(i, j)]
-            ups_done.append(push(up, heads.at[3, shard(i, j)], ups.at[n], upr.at[n], y_next))
+            push(up, heads.at[3, shard(i, j)], ups.at[0], upr.at[0], y_next, True)
 
     def spread(k, i):
         for side, step in enumerate((1, 3, 2) if k == 0 else (1, 3)):
             device = (shard(0, step), s)
-            p2[k, i, side] = along(k, i, 0, full, p2s.at[k, i, side], p2r.at[k, i, side], device)
+            p2[k, i, side] = along(k, i, 0, full, p2s.at[0], p2r.at[k, i, side], device)
         to_y(k, i, 0)
 
     def hop(k):
         for side, step in enumerate((1, 3, 2)):
             device = (shard(step, 0), s)
-            p1[k, side] = along(k, 0, 0, full, p1s.at[k, side], p1r.at[k, side], device)
+            p1[k, side] = along(k, 0, 0, full, p1s.at[0], p1r.at[k, side], device)
 
     def hop_end(k):
         for side in range(3):
@@ -229,7 +264,7 @@
             step = (1, 3)[side]
             p2[k, i, side].wait_recv()
             device = (shard(0, step), s)
-            p2[k, i, 2] = along(k, i, 4 - step, full, p2s.at[k, i, 2], p2r.at[k, i, 2], device)
+            p2[k, i, 2] = along(k, i, 4 - step, full, p2s.at[0], p2r.at[k, i, 2], device)
             p2[k, i, 1 - side].wait_recv()
 
     def event4(k):
@@ -244,6 +279,8 @@
     hop(1)
     hop(2)
 
+    for load in loads[:12]:
+        load.wait()
     feats = feat_ref[...]
     feats32 = feats.astype(F32)
     cross = nn(feats, w_cross_ref[...]) + b_cross_ref[...].astype(F32).reshape(1, 512)
@@ -255,7 +292,7 @@
     scores[...] = jnp.broadcast_to(b_score_ref[...].astype(F32), scores.shape)
     table_pad[...] = jnp.zeros_like(table_pad)
     table_pad[0:16] = table_ref[...]
-    loads[2].wait()
+    loads[14].wait()
 
     def embed(i):
         rows = slice(i * 256, i * 256 + 256)
@@ -280,8 +317,8 @@
         hid_t[cols, :] = hidden.T
         scores[...] += nn(hidden, w_score_ref[cols, :])
 
-    loads[0].wait()
-    loads[1].wait()
+    loads[12].wait()
+    loads[13].wait()
     for j in range(2):
         forward(j)
     for k in (1, 2):
@@ -351,25 +388,21 @@
     place_out[:, :CAP] = placed
     place_out[:, CAP:] = jnp.broadcast_to(own_half[mine_rows, :][None], (16, 32, 128))
     rows_in[t] = place_out[t]
-    row_copies = []
-    for k in range(1, 16):
-        to = (t + k) % 16
-        row_copies.append(push(place_out.at[to], rows_in.at[t], srs.at[k], srr.at[k], (to, s)))
-
     event3(1)
     for copy in (hist_copy, picked_copy, mask_copy):
         copy.wait_recv()
     attend(0, functools.partial(event3, 2))
+    for k in range(1, 16):
+        to = (t + k) % 16
+        push(place_out.at[to], rows_in.at[t], srs.at[0], srr.at[0], (to, s), True)
     event4(1)
     attend(1, functools.partial(event4, 2))
-    for copy in row_copies:
-        copy.wait_recv()
+    whole_of(rows_in.at[0:15], srs.at[0], srr.at[0]).wait_recv()
     out_head[:, mine_rows] = rows_in[:, CAP:]
     every = out_head.at[:, mine_rows]
     oh_sib = push(every, every, ohs.at[0], ohr.at[0], sibling)
     attend(2)
-    for copy in ups_done:
-        copy.wait_recv()
+    whole_of(heads.at[3], ups.at[0], upr.at[0]).wait_recv()
     attend(3)
     for copy in att_done:
         copy.wait_recv()
@@ -431,8 +464,8 @@
         right, left, opp = (m + 1) % 4, (m + 3) % 4, (m + 2) % 4
         to_right, to_left = at_chip(axis, right, c), at_chip(axis, left, c)
         return (
-            push(grads.at[piece(u, opp, 0)], x1.at[u, 0], s1s.at[u, 0], s1r.at[u, 0], to_right),
-            push(grads.at[piece(u, opp, 1)], x1.at[u, 1], s1s.at[u, 1], s1r.at[u, 1], to_left),
+            push(grads.at[piece(u, opp, 0)], x1.at[u, 0], s1s.at[0], s1r.at[u, 0], to_right, True),
+            push(grads.at[piece(u, opp, 1)], x1.at[u, 1], s1s.at[0], s1r.at[u, 1], to_left, True),
         )
 
     def stage1_second(u):
@@ -441,8 +474,8 @@
         right, left = (m + 1) % 4, (m + 3) % 4
         to_right, to_left = at_chip(axis, right, c), at_chip(axis, left, c)
         return (
-            push(grads.at[piece(u, right, 1)], x2.at[u, 0], s1s.at[u, 2], s1r.at[u, 2], to_right),
-            push(grads.at[piece(u, left, 0)], x2.at[u, 1], s1s.at[u, 3], s1r.at[u, 3], to_left),
+            push(grads.at[piece(u, right, 1)], x2.at[u, 0], s1s.at[1], s1r.at[u, 2], to_right, True),
+            push(grads.at[piece(u, left, 0)], x2.at[u, 1], s1s.at[1], s1r.at[u, 3], to_left, True),
         )
 
     def stage1_pass(u, started):
@@ -457,7 +490,7 @@
             mine = grads[piece(u, where, side)].astype(F32)
             y3[u, side] = (mine + x1[u, side].astype(F32)).astype(BF)
             out.append(
-                push(y3.at[u, side], x3.at[u, side], s1s.at[u, 4 + side], s1r.at[u, 4 + side], device)
+                push(y3.at[u, side], x3.at[u, side], s1s.at[2], s1r.at[u, 4 + side], device, True)
             )
         return out
 
@@ -524,9 +557,10 @@
             push(
                 w1.at[piece2(u, (m + step) % 4)],
                 v1.at[u, k],
-                s2s.at[u, k],
+                s2s.at[0],
                 s2r.at[u, k],
                 at_chip(axis, (m + step) % 4, c),
+                True,
             )
             for k, step in enumerate((1, 3, 2))
         ]
@@ -551,28 +585,13 @@
                 push(
                     w2.at[r, :, where],
                     last.at[r, m, c],
-                    s3s.at[r, k, other],
-                    s3r.at[r, k, other],
+                    s3s.at[k],
+                    s3r.at[k],
                     at_chip(axis, where, core),
+                    True,
                 )
 
     def stage3_end(r):
-        axis = ROUTES[r][2]
-        m = pos[axis]
-        for k in range(4):
-            where = (m + 4 - k) % 4
-            for other in range(2):
-                if k == 0 and other == 0:
-                    continue
-                core = c if other == 0 else 1 - c
-                pltpu.make_async_remote_copy(
-                    src_ref=last.at[r, where, core],
-                    dst_ref=last.at[r, where, core],
-                    send_sem=s3s.at[r, k, other],
-                    recv_sem=s3r.at[r, k, other],
-                    device_id=at_chip(axis, where, core),
-                    device_id_type=MESH,
-                ).wait_recv()
         scale = 1.0 / 32768.0
         for core in range(2):
             total = last[r, 0, core].astype(F32)
@@ -589,6 +608,10 @@
             stage2_end(u, begun[u])
         stage3_start(r)
     o_rows[...] = rows_in[:, :CAP]
+    stage3_all = [whole_of(last.at[:, 0, 0], s3s.at[0], s3r.at[0])]
+    stage3_all += [whole_of(last.at[:, 0], s3s.at[k], s3r.at[k]) for k in range(1, 4)]
+    for copy in stage3_all:
+        copy.wait_recv()
     for r in range(3):
         stage3_end(r)
 
@@ -611,6 +634,15 @@
     bias = fin[0, 5, 0:8, 128:256] + fin[1, 5, 0:8, 128:256]
     for row, first in enumerate((chip % 2 * 64 + c * 32, chip % 16 * 8 + c * 4, chip * 2 + c)):
         o_bias[row : row + 1] = pltpu.roll(bias, (128 - first) % 128, 1)[row : row + 1]
+    sends += stage3_all
+    sends.append(whole_of(heads.at[0, 0:9], p1s.at[0], upr.at[0]))
+    sends.append(whole_of(heads.at[0:3, 0:12], p2s.at[0], upr.at[0]))
+    sends.append(whole_of(heads.at[0], ups.at[0], upr.at[0]))
+    sends.append(whole_of(place_out.at[0:15], srs.at[0], srr.at[0]))
+    sends.append(whole_of(x1, s1s.at[0], upr.at[0]))
+    sends.append(whole_of(x2, s1s.at[1], upr.at[0]))
+    sends.append(whole_of(x3, s1s.at[2], upr.at[0]))
+    sends.append(whole_of(v1, s2s.at[0], upr.at[0]))
     for copy in sends:
         copy.wait_send()
 
@@ -657,9 +689,21 @@
             jax.ShapeDtypeStruct((8, 128), F32),
             jax.ShapeDtypeStruct((16, CAP, 128), BF),
         ),
-        in_specs=[stay] + [whole] * 6 + [stay] * 2 + [whole] * 4 + [stay, whole, stay, whole],
+        in_specs=[stay] * 17,
         out_specs=(whole,) * 5,
         scratch_shapes=[
+            vmem((1, 1024), jnp.int32),
+            vmem((1, 1024), jnp.int32),
+            vmem((1, 256), jnp.int32),
+            vmem((1, 256), jnp.int32),
+            vmem((256, 512), BF),
+            vmem((16, 1024), BF),
+            vmem((64, 1024), BF),
+            vmem((1024, 128), BF),
+            vmem((512, 512), BF),
+            vmem((512,), BF),
+            vmem((4096,), BF),
+            vmem((1, 128), BF),
             vmem((1024, 1024), BF),
             vmem((512, 4096), BF),
             vmem((4096, 128), BF),
@@ -704,24 +748,24 @@
             vmem((3, 2, 4, 16, 256), BF),
             vmem((3, 4, 2, 2, 16, 256), BF),
             vmem((2, 6, 16, 256), F32),
+            dma((3,)),
             dma((6, 6)),
-            dma((6, 6)),
+            dma((1,)),
             dma((6, 3)),
-            dma((6, 3)),
-            dma((3, 4, 2)),
-            dma((3, 4, 2)),
+            dma((4,)),
+            dma((4,)),
             dma((8,)),
             dma((8,)),
-            dma((16,)),
-            dma((16,)),
-            dma((3,)),
+            dma((1,)),
+            dma((1,)),
+            dma((15,)),
             dma((3, 4)),
-            dma((3, 4)),
-            dma((3, 4)),
+            dma((1,)),
+            dma((3, 3)),
+            dma((1,)),
             dma((3, 4, 3)),
-            dma((3, 4, 3)),
-            dma((16,)),
-            dma((16,)),
+            dma((1,)),
+            dma((1,)),
             dma((11,)),
             dma((11,)),
             dma((1,)),

time: 72.5 us -> 69.3 us (0.956)
  Pallas kernels: 71.7 us -> 68.5 us
    pallas_call x1, Pallas kernels: 70 us -> 66.8 us  [local(): pl.pallas_call(kernel, out_shape=(jax.ShapeDtypeStruct((4, 512), F32), ja...]
where the time goes in v1:
time: 69.3 us; the launch traced here: 69.2 us
  Pallas kernels  68.5 us (99%)
    pallas_call x1, Pallas kernels, local(): pl.pallas_call(kernel, out_shape=(jax.ShapeDtypeStruct((4, 512), F32), ja...  66.8 us
    pallas_call x1, Pallas kernels, local(): pl.pallas_call(results, out_shape=(jax.ShapeDtypeStruct((4, 512), F32), j...  1.69 us

profile of v1, /device:TPU:1, one launch (start us, length us, event | category | flops | bytes accessed | tf_op | source)
XLA Modules:
  0.0 69.2 jit_solution(7870603762570559164)
XLA Ops:
  0.6 66.8 %shard_map.216 = (f32[4,512]{1,0:T(4,128)}, f32[4,4096]{1,0:T(4,128)}, f32[32,128]{1,0:T(8,128)}, f32[8,128]{1,0:T(8,128)}, bf16[16,32,128]{2,1,0:T(8,128)(2,1)}) custom-call(bf16[1024,1024]{1,0:T(8,128)(2,1)} %emb_hbm.1, s32[1,1024]{1,0:T(1,128)} %bitcast.6, s32[1,1024]{1,0:T(1,128)} %segs_hbm.1, s32[1,256]{1,0:T(1,128)} %bitcast.7, s32[1,256]{1,0:T(1,128)} %bitcast.8, ...), custom_call_target="tpu_custom_call" | custom-call | tf_op jit(solution)/shard_map/pallas_call | solution.py:683
  67.5 1.7 %shard_map.217 = (f32[4,512]{1,0:T(4,128)}, f32[4]{0:T(128)}, f32[4,4096]{1,0:T(4,128)}, f32[32]{0:T(128)}, f32[32,128]{1,0:T(8,128)}, /*index=5*/f32[1]{0:T(128)}, bf16[512,128]{1,0:T(8,128)(2,1)}) custom-call(f32[4,512]{1,0:T(4,128)} %get-tuple-element.12.cross, f32[4,4096]{1,0:T(4,128)} %get-tuple-element.13.deep, f32[32,128]{1,0:T(8,128)} %get-tuple-element.14.score, ...), custom_call_target="tpu_custom_call" | custom-call | tf_op jit(solution)/shard_map/pallas_call | solution.py:796

commit v2 on v1

--- a/solution.py
+++ b/solution.py
@@ -172,9 +172,8 @@
             device_id_type=MESH,
         )
 
-    peers = [((t + k) % 16, s) for k in range(1, 16)] + [sibling]
-    peers += [at_chip(2, (y + k) % 4, c) for k in range(1, 4)]
-    peers += [at_chip(axis, (pos[axis] + k) % 4, 1 - c) for axis in range(3) for k in range(1, 4)]
+    peers = [at_chip(axis, (pos[axis] + k) % 4, c) for axis in (0, 1) for k in (1, 2, 3)]
+    peers += [at_chip(2, (y + k) % 4, c) for k in (1, 3)] + [sibling]
     barrier = pltpu.get_barrier_semaphore()
     for peer in peers:
         pl.semaphore_signal(barrier, inc=1, device_id=peer, device_id_type=MESH)
@@ -433,19 +432,6 @@
         d_copies[q] = push(d_own.at[j], d_sib.at[q], scs.at[2 + q], scr.at[2 + q], sibling)
     for q in (0, 1, 3, 2):
         back_chunk(c * 4 + q)
-    for i in range(8):
-        g = nn(hid_t[512 * i : 512 * i + 512, :], delta16).astype(BF).reshape(8, 2, 2, 16, 128)
-        for core in range(2):
-            gs[core, 8 * i : 8 * i + 8, :, 0:128] = g[:, core, 0]
-            gs[core, 8 * i : 8 * i + 8, :, 128:256] = g[:, core, 1]
-    gs_copy = push(gs.at[1 - c], gs_sib, scs.at[6], scr.at[6], sibling)
-    every_dpre = jnp.concatenate([d_own[j] for j in range(8)], axis=1)
-    dcr = nt(every_dpre, w_deep_ref[...]) * feats32
-    bcross = jnp.sum(dcr, axis=0, keepdims=True)
-    dc[0] = dcr[:, :256].astype(BF)
-    dc[1] = dcr[:, 256:].astype(BF)
-    dc_copy = push(dc.at[1 - c], dc_sib, scs.at[7], scr.at[7], sibling)
-
     def axes_of(u):
         axis = ROUTES[u // 2][0]
         rest = [a for a in range(3) if a != axis]
@@ -507,13 +493,30 @@
     started, passed = {}, {}
 
     ct_copy.wait_recv()
-    for q in (0, 1, 3, 2):
+
+    def deep_unit(q):
         d_copies[q].wait_recv()
         g = nn(ct[...], d_own[c * 4 + q]) + nn(ct_sib[...], d_sib[q])
         g = g.reshape(64, 8, 512)
         g = jnp.concatenate([g[:, :, :256], g[:, :, 256:]], axis=1)
         grads[1 + q] = g.astype(BF).reshape(4, 4, 4, 16, 256)
         started[1 + q] = stage1_first(1 + q)
+
+    for q in (0, 1, 3):
+        deep_unit(q)
+    for i in range(8):
+        g = nn(hid_t[512 * i : 512 * i + 512, :], delta16).astype(BF).reshape(8, 2, 2, 16, 128)
+        for core in range(2):
+            gs[core, 8 * i : 8 * i + 8, :, 0:128] = g[:, core, 0]
+            gs[core, 8 * i : 8 * i + 8, :, 128:256] = g[:, core, 1]
+    gs_copy = push(gs.at[1 - c], gs_sib, scs.at[6], scr.at[6], sibling)
+    every_dpre = jnp.concatenate([d_own[j] for j in range(8)], axis=1)
+    dcr = nt(every_dpre, w_deep_ref[...]) * feats32
+    bcross = jnp.sum(dcr, axis=0, keepdims=True)
+    dc[0] = dcr[:, :256].astype(BF)
+    dc[1] = dcr[:, 256:].astype(BF)
+    dc_copy = push(dc.at[1 - c], dc_sib, scs.at[7], scr.at[7], sibling)
+    deep_unit(2)
 
     gs_copy.wait_recv()
     summed = gs[c].astype(F32) + gs_sib[...].astype(F32)

time: 69.3 us -> 68.5 us (0.988)
  Pallas kernels: 68.5 us -> 67.7 us
    pallas_call x1, Pallas kernels: 66.8 us -> 66 us  [local(): pl.pallas_call(kernel, out_shape=(jax.ShapeDtypeStruct((4, 512), F32), ja...]
where the time goes in v2:
time: 68.5 us; the launch traced here: 68.4 us
  Pallas kernels  67.7 us (99%)
    pallas_call x1, Pallas kernels, local(): pl.pallas_call(kernel, out_shape=(jax.ShapeDtypeStruct((4, 512), F32), ja...  66 us
    pallas_call x1, Pallas kernels, local(): pl.pallas_call(results, out_shape=(jax.ShapeDtypeStruct((4, 512), F32), j...  1.69 us

profile of v2, /device:TPU:1, one launch (start us, length us, event | category | flops | bytes accessed | tf_op | source)
XLA Modules:
  0.0 68.4 jit_solution(14879733713862510565)
XLA Ops:
  0.6 66.0 %shard_map.216 = (f32[4,512]{1,0:T(4,128)}, f32[4,4096]{1,0:T(4,128)}, f32[32,128]{1,0:T(8,128)}, f32[8,128]{1,0:T(8,128)}, bf16[16,32,128]{2,1,0:T(8,128)(2,1)}) custom-call(bf16[1024,1024]{1,0:T(8,128)(2,1)} %emb_hbm.1, s32[1,1024]{1,0:T(1,128)} %bitcast.6, s32[1,1024]{1,0:T(1,128)} %segs_hbm.1, s32[1,256]{1,0:T(1,128)} %bitcast.7, s32[1,256]{1,0:T(1,128)} %bitcast.8, ...), custom_call_target="tpu_custom_call" | custom-call | tf_op jit(solution)/shard_map/pallas_call | solution.py:686
  66.7 1.7 %shard_map.217 = (f32[4,512]{1,0:T(4,128)}, f32[4]{0:T(128)}, f32[4,4096]{1,0:T(4,128)}, f32[32]{0:T(128)}, f32[32,128]{1,0:T(8,128)}, /*index=5*/f32[1]{0:T(128)}, bf16[512,128]{1,0:T(8,128)(2,1)}) custom-call(f32[4,512]{1,0:T(4,128)} %get-tuple-element.12.cross, f32[4,4096]{1,0:T(4,128)} %get-tuple-element.13.deep, f32[32,128]{1,0:T(8,128)} %get-tuple-element.14.score, ...), custom_call_target="tpu_custom_call" | custom-call | tf_op jit(solution)/shard_map/pallas_call | solution.py:799

commit v3 on v2

--- a/solution.py
+++ b/solution.py
@@ -395,14 +395,15 @@
         to = (t + k) % 16
         push(place_out.at[to], rows_in.at[t], srs.at[0], srr.at[0], (to, s), True)
     event4(1)
-    attend(1, functools.partial(event4, 2))
+    attend(1)
+    whole_of(heads.at[3], ups.at[0], upr.at[0]).wait_recv()
+    attend(3)
     whole_of(rows_in.at[0:15], srs.at[0], srr.at[0]).wait_recv()
     out_head[:, mine_rows] = rows_in[:, CAP:]
     every = out_head.at[:, mine_rows]
     oh_sib = push(every, every, ohs.at[0], ohr.at[0], sibling)
+    event4(2)
     attend(2)
-    whole_of(heads.at[3], ups.at[0], upr.at[0]).wait_recv()
-    attend(3)
     for copy in att_done:
         copy.wait_recv()
 

time: 68.5 us -> 66.8 us (0.975)
  Pallas kernels: 67.7 us -> 66.1 us
    pallas_call x1, Pallas kernels: 66 us -> 64.4 us  [local(): pl.pallas_call(kernel, out_shape=(jax.ShapeDtypeStruct((4, 512), F32), ja...]
where the time goes in v3:
time: 66.8 us; the launch traced here: 66.7 us
  Pallas kernels  66.1 us (99%)
    pallas_call x1, Pallas kernels, local(): pl.pallas_call(kernel, out_shape=(jax.ShapeDtypeStruct((4, 512), F32), ja...  64.4 us
    pallas_call x1, Pallas kernels, local(): pl.pallas_call(results, out_shape=(jax.ShapeDtypeStruct((4, 512), F32), j...  1.69 us

profile of v3, /device:TPU:1, one launch (start us, length us, event | category | flops | bytes accessed | tf_op | source)
XLA Modules:
  0.0 66.7 jit_solution(2441848198792439202)
XLA Ops:
  0.6 64.4 %shard_map.216 = (f32[4,512]{1,0:T(4,128)}, f32[4,4096]{1,0:T(4,128)}, f32[32,128]{1,0:T(8,128)}, f32[8,128]{1,0:T(8,128)}, bf16[16,32,128]{2,1,0:T(8,128)(2,1)}) custom-call(bf16[1024,1024]{1,0:T(8,128)(2,1)} %emb_hbm.1, s32[1,1024]{1,0:T(1,128)} %bitcast.6, s32[1,1024]{1,0:T(1,128)} %segs_hbm.1, s32[1,256]{1,0:T(1,128)} %bitcast.7, s32[1,256]{1,0:T(1,128)} %bitcast.8, ...), custom_call_target="tpu_custom_call" | custom-call | tf_op jit(solution)/shard_map/pallas_call | solution.py:687
  65.0 1.7 %shard_map.217 = (f32[4,512]{1,0:T(4,128)}, f32[4]{0:T(128)}, f32[4,4096]{1,0:T(4,128)}, f32[32]{0:T(128)}, f32[32,128]{1,0:T(8,128)}, /*index=5*/f32[1]{0:T(128)}, bf16[512,128]{1,0:T(8,128)(2,1)}) custom-call(f32[4,512]{1,0:T(4,128)} %get-tuple-element.12.cross, f32[4,4096]{1,0:T(4,128)} %get-tuple-element.13.deep, f32[32,128]{1,0:T(8,128)} %get-tuple-element.14.score, ...), custom_call_target="tpu_custom_call" | custom-call | tf_op jit(solution)/shard_map/pallas_call | solution.py:800
